TPU v7x, 128 devices: a whole 4x4x4 slice. The times are simulated.
128 devices in a mesh: batch: 4 (over x_lo, core), patch: 32 (over y, z, x_hi).
Axes of the slice: x: 4 (x_hi: 2, x_lo: 2; x = x_hi * 2 + x_lo), y: 4, z: 4, core: 2. Of those that a mesh axis runs over, the one named last changes fastest.
Arguments:
- latent: bfloat16 [512, 64, 1280], P(('batch', 'patch')), parts along dimension 0, may hold values from -30 to 30
- gn_gain: float32 [1280], replicated, may hold values from 0.1 to 1.9
- w_query: bfloat16 [1280, 640], replicated, may hold values from -0.15625 to 0.15625
- w_key: bfloat16 [1280, 640], replicated, may hold values from -0.15625 to 0.15625
- w_value: bfloat16 [1280, 640], replicated, may hold values from -0.15625 to 0.15625
- w_out: bfloat16 [640, 1280], replicated, may hold values from -0.25 to 0.25
- stale_keys: bfloat16 [32768, 640], P(('batch', 'patch')), parts along dimension 0, may hold values from -150 to 150
- stale_values: bfloat16 [32768, 640], P(('batch', 'patch')), parts along dimension 0, may hold values from -5 to 5
- gn2_gain: float32 [1280], replicated, may hold values from 0.1 to 1.9
- conv_weight: bfloat16 [9, 1280, 640], replicated, may hold values from -0.0546875 to 0.0546875
- time_shift: float32 [2560], P('batch'), parts along dimension 0, may hold values from -4 to 4
Outputs:
- result: bfloat16 [512, 64, 640], P(('batch', 'patch')), parts along dimension 0
- fresh_keys: bfloat16 [32768, 640], P(('batch', 'patch')), parts along dimension 0
- fresh_values: bfloat16 [32768, 640], P(('batch', 'patch')), parts along dimension 0
There are 4 independent parts, one for each index of `batch`. A program takes and returns all parts, laid end to end along the dimension named above; an argument that names none is the same for every part. Nothing has to cross between parts.
All inputs are finite; a program needn't handle non-finite values.
Results may differ from a plain program's by a relative error of at most 0.005.
The roundings to bfloat16 on the way count: a program that leaves them out, or rounds other values in their place, can miss the bound.
Values may be sent and summed in bfloat16 or wider, within the bound.
No kernel may reach another device: no remote copies, remote signals or barrier semaphores. Data moves between devices by JAX's collectives and lax.ppermute only.
A program may use at most 128 MiB of HBM per device.

v0:
```python
import jax
import jax.numpy as jnp
from jax import lax
from jax.sharding import PartitionSpec as P

HEAD = 64
HEADS = 10
GROUPS = 32


def padded_2(x, sides, width):
    for axis, dim in sides:
        peers, length = (lax.axis_size(axis), x.shape[dim])
        up = [(i, (i + 1) % peers) for i in range(peers - 1)]
        down = [(j, i) for i, j in up]
        last = lax.slice_in_dim(x, length - width, length, axis=dim)
        initial = lax.slice_in_dim(x, 0, width, axis=dim)
        before = lax.ppermute(last, axis, up)
        after = lax.ppermute(initial, axis, down)
        x = jnp.concatenate([before, x, after], axis=dim)
    return x


def group_norm(features, gain):
    row_count, col_count, channels = features.shape
    grouped = features.reshape(row_count * col_count, GROUPS, channels // GROUPS)
    members = row_count * col_count * (channels // GROUPS) * lax.axis_size("patch")
    totals = lax.psum(jnp.sum(grouped, axis=(0, 2)), "patch")
    center = totals / members
    spread = lax.psum(jnp.sum(jnp.square(grouped - center[None, :, None]), axis=(0, 2)), "patch")
    variance = spread / members
    scaled = (grouped - center[None, :, None]) * lax.rsqrt(variance + 1e-05)[None, :, None]
    return scaled.reshape(features.shape) * gain


def scores_of(q_heads, key_block):
    return (
        jnp.einsum("qhd,khd->qhk", q_heads, key_block, preferred_element_type=jnp.float32) * 0.125
    )


def own_block(q_heads, key_block, value_block):
    scores = scores_of(q_heads, key_block)
    top = jnp.max(scores, axis=2)
    weights = jnp.exp(scores - top[..., None])
    totals = jnp.sum(weights, axis=2)
    summed = jnp.einsum(
        "qhk,khd->qhd",
        weights.astype(jnp.bfloat16),
        value_block,
        preferred_element_type=jnp.float32,
    )
    return (top, totals, summed)


def absorb(state, q_heads, key_block, value_block, valid):
    top, totals, summed = state
    scores = scores_of(q_heads, key_block)
    scores = jnp.where(valid[None, None, :], scores, -jnp.inf)
    new_top = jnp.maximum(top, jnp.max(scores, axis=2))
    weights = jnp.exp(scores - new_top[..., None])
    factor = jnp.exp(top - new_top)
    totals = totals * factor + jnp.sum(weights, axis=2)
    summed = summed * factor[..., None] + jnp.einsum(
        "qhk,khd->qhd",
        weights.astype(jnp.bfloat16),
        value_block,
        preferred_element_type=jnp.float32,
    )
    return (new_top, totals, summed)


def shards(
    latent,
    gn_gain,
    w_query,
    w_key,
    w_value,
    w_out,
    stale_keys,
    stale_values,
    gn2_gain,
    conv_weight,
    time_shift,
):
    row_count, col_count, channels = latent.shape
    tok_count = row_count * col_count
    features = latent.astype(jnp.float32)
    normed = group_norm(features, gn_gain).astype(jnp.bfloat16).reshape(tok_count, channels)
    queries = jnp.dot(normed, w_query, preferred_element_type=jnp.float32).astype(jnp.bfloat16)
    fresh_keys = jnp.dot(normed, w_key, preferred_element_type=jnp.float32).astype(jnp.bfloat16)
    fresh_values = jnp.dot(normed, w_value, preferred_element_type=jnp.float32).astype(jnp.bfloat16)
    own_index = lax.axis_index("patch")
    q_heads = queries.reshape(tok_count, HEADS, HEAD)
    state = own_block(
        q_heads,
        fresh_keys.reshape(tok_count, HEADS, HEAD),
        fresh_values.reshape(tok_count, HEADS, HEAD),
    )
    key_piece = lax.all_gather(stale_keys, "patch", axis=0, tiled=True)
    value_piece = lax.all_gather(stale_values, "patch", axis=0, tiled=True)
    length = key_piece.shape[0]

    def advance(block_no, carried):
        offset = block_no * tok_count
        key_block = lax.dynamic_slice_in_dim(key_piece, offset, tok_count, 0).reshape(
            tok_count, HEADS, HEAD
        )
        value_block = lax.dynamic_slice_in_dim(value_piece, offset, tok_count, 0).reshape(
            tok_count, HEADS, HEAD
        )
        positions = offset + jnp.arange(tok_count, dtype=jnp.int32)
        valid = positions // tok_count != own_index
        return absorb(carried, q_heads, key_block, value_block, valid)

    state = lax.fori_loop(0, length // tok_count, advance, state)
    top, totals, summed = state
    attended = (summed / totals[..., None]).astype(jnp.bfloat16).reshape(tok_count, HEADS * HEAD)
    mixed = jnp.dot(attended, w_out, preferred_element_type=jnp.float32).reshape(
        row_count, col_count, channels
    )
    hidden = features + mixed
    activated = jax.nn.silu(group_norm(hidden, gn2_gain)).astype(jnp.bfloat16)
    padded = padded_2(activated, (("patch", 0),), 1)
    padded = jnp.pad(padded, ((0, 0), (1, 1), (0, 0)))
    out_width = conv_weight.shape[2]
    conv_sum = jnp.zeros((tok_count, out_width), jnp.float32)
    for tap_row in range(3):
        for tap_col in range(3):
            window = padded[tap_row : tap_row + row_count, tap_col : tap_col + col_count].reshape(
                tok_count, channels
            )
            conv_sum = conv_sum + jnp.dot(
                window, conv_weight[3 * tap_row + tap_col], preferred_element_type=jnp.float32
            )
    result = (
        hidden[..., :out_width] + conv_sum.reshape(row_count, col_count, out_width) + time_shift
    )
    return (result.astype(jnp.bfloat16), fresh_keys, fresh_values)


def solution(mesh):
    placed = (
        P(("batch", "patch"), None, None),
        P(),
        P(),
        P(),
        P(),
        P(),
        P(("batch", "patch"), None),
        P(("batch", "patch"), None),
        P(),
        P(),
        P("batch"),
    )
    return jax.shard_map(
        shards,
        mesh=mesh,
        in_specs=placed,
        out_specs=(
            P(("batch", "patch"), None, None),
            P(("batch", "patch"), None),
            P(("batch", "patch"), None),
        ),
        check_vma=False,
    )
```

profile of v0, /device:TPU:0, one launch (start us, length us, event | category | flops | bytes accessed | tf_op | source)
XLA Modules:
  0.0 573.9 jit_solution(14737773272477465279)
XLA Ops:
  7.2 2.0 copy.36
  9.3 1.9 copy.37
  11.6 99.2 %psum.28 = f32[32]{0:T(128)S(1)} all-reduce(f32[32]{0:T(128)S(1)} %reduce_sum.91), channel_id=1, replica_groups=mesh['batch'=4,'patch'=32] {'patch'}, use_global_device_ids=true, to_apply=%region_2.0 | all-reduce | flops 32 | bytes 256 | tf_op jit(solution)/shard_map/psum | solution.py:28
  111.4 90.1 %psum.29 = f32[32]{0:T(128)S(1)} all-reduce(f32[32]{0:T(128)S(1)} %reduce_sum.94), channel_id=1, replica_groups=mesh['batch'=4,'patch'=32] {'patch'}, use_global_device_ids=true, to_apply=%region_5.0 | all-reduce | flops 32 | bytes 256 | tf_op jit(solution)/shard_map/psum | solution.py:30
  201.8 2.1 convolution_convert_fusion.1
  204.1 2.1 convolution_convert_fusion.2
  206.5 2.9 convolution_convert_fusion
  209.3 1.1 copy.34
  212.1 28.0 %all-gather.5.cloned.1.call-done = bf16[8192,640]{0,1:T(8,128)(2,1)} async-done(((bf16[256,640]{0,1:T(8,128)(2,1)}), bf16[8192,640]{0,1:T(8,128)(2,1)}) %all-gather.5.cloned.1.call-update) | async-done | bytes 10485776 | tf_op jit(solution)/shard_map/all_gather | solution.py:101
  240.1 106.0 %while.19 = (s32[]{:T(128)}, f32[256,10]{0,1:T(8,128)S(1)}, f32[256,10]{0,1:T(8,128)S(1)}, f32[256,10,64]{0,2,1:T(8,128)S(1)}, s32[]{:T(128)}, /*index=5*/bf16[8...) while((s32[]{:T(128)}, f32[256,10]{0,1:T(8,128)S(1)}, ...), condition=%wide.region_11.12_spmd, body=%wide.region_8.0_spmd.sunk | while | flops 175318272 | bytes 11633839 | solution.py:116
  243.4 1.1 constant_dynamic-slice_fusion.3
  250.1 1.1 constant_dynamic-slice_fusion.3
  253.4 1.1 constant_dynamic-slice_fusion.3
  263.3 1.1 constant_dynamic-slice_fusion.3
  273.3 1.1 constant_dynamic-slice_fusion.3
  276.6 1.1 constant_dynamic-slice_fusion.3
  279.9 1.1 constant_dynamic-slice_fusion.3
  283.2 1.1 constant_dynamic-slice_fusion.3
  286.5 1.1 constant_dynamic-slice_fusion.3
  289.8 1.1 constant_dynamic-slice_fusion.3
  293.1 1.1 constant_dynamic-slice_fusion.3
  296.4 1.1 constant_dynamic-slice_fusion.3
  299.8 1.1 constant_dynamic-slice_fusion.3
  303.1 1.1 constant_dynamic-slice_fusion.3
  306.4 1.1 constant_dynamic-slice_fusion.3
  309.7 1.1 constant_dynamic-slice_fusion.3
  313.0 1.1 constant_dynamic-slice_fusion.3
  316.3 1.1 constant_dynamic-slice_fusion.3
  319.6 1.1 constant_dynamic-slice_fusion.3
  326.3 1.1 constant_dynamic-slice_fusion.3
  329.6 1.1 constant_dynamic-slice_fusion.3
  336.2 1.1 constant_dynamic-slice_fusion.3
  346.2 1.1 dot_general.72
  347.3 2.0 fusion.97
  349.5 94.2 %psum.30 = f32[32]{0:T(128)S(1)} all-reduce(f32[32]{0:T(128)S(1)} %reduce_sum.98), channel_id=1, replica_groups=mesh['batch'=4,'patch'=32] {'patch'}, use_global_device_ids=true, to_apply=%region_14.15 | all-reduce | flops 32 | bytes 256 | tf_op jit(solution)/shard_map/psum | solution.py:28
  444.3 89.2 %psum.31 = f32[32]{0:T(128)S(1)} all-reduce(f32[32]{0:T(128)S(1)} %reduce_sum.101), channel_id=1, replica_groups=mesh['batch'=4,'patch'=32] {'patch'}, use_global_device_ids=true, to_apply=%region_17.18 | all-reduce | flops 32 | bytes 256 | tf_op jit(solution)/shard_map/psum | solution.py:30
  534.1 5.4 collective-permute-start
  539.5 1.5 collective-permute-start.1
  540.9 2.1 fusion.30
  543.1 5.1 collective-permute-done.1
  548.3 2.1 fusion.24
  551.2 2.1 fusion.38
  553.3 2.1 fusion.26
  555.5 2.1 fusion.28
  557.6 2.1 fusion.32
  559.7 2.1 fusion.34
  561.8 2.1 fusion.22
  564.0 2.3 fusion.86
  (288 shorter events, 85.3 us)
Async XLA Ops:
  7.2 340.1 %copy-start = (bf16[640,1280]{1,0:T(8,128)(2,1)S(1)}, bf16[640,1280]{1,0:T(8,128)(2,1)}, u32[]{:S(2)}) copy-start(bf16[640,1280]{1,0:T(8,128)(2,1)} %param.18) | copy-start | bytes 4915204
  7.2 4.1 copy-start.1
  7.2 194.4 %copy-start.3 = (f32[1280]{0:T(1024)S(1)}, f32[1280]{0:T(1024)}, u32[]{:S(2)}) copy-start(f32[1280]{0:T(1024)} %param.14) | copy-start | bytes 15364
  7.2 204.9 %all-gather.3.cloned.1.call-start = ((), (), s32[]{:S(2)}) async-start(), calls=%async_computation | async-start | bytes 10813440 | tf_op jit(solution)/shard_map/all_gather | solution.py:100
  9.3 230.8 %all-gather.5.cloned.1.call-start = ((), (), s32[]{:S(2)}) async-start(), calls=%async_computation.1 | async-start | bytes 10813440 | tf_op jit(solution)/shard_map/all_gather | solution.py:101
  206.3 3.1 copy-start.2
  347.3 186.3 %copy-start.4 = (f32[1280]{0:T(1024)S(1)}, f32[1280]{0:T(1024)}, u32[]{:S(2)}) copy-start(f32[1280]{0:T(1024)} %param.21) | copy-start | bytes 15364
  534.1 9.0 %collective-permute-start = (bf16[1,64,1280]{2,1,0:T(8,128)(2,1)S(1)}, bf16[1,64,1280]{2,1,0:T(8,128)(2,1)S(1)}, u32[]{:S(2)}, u32[]{:S(2)}) collective-permute-start(bf16[1,64,1280]{2,1,0:T(8,128)(2,1)S(1)} %get-tuple-element.243), channel_id=1, source_target_pairs={{0,1},{1,2},{2,3},{3,4},{4,5},{5,6},{6,7},{7,8},{8,9},{9,10},{10,1... | collective-permute-start | bytes 491528 | tf_op jit(solution)/shard_map/ppermute | solution.py:18
  539.5 8.7 %collective-permute-start.1 = (bf16[1,64,1280]{2,1,0:T(8,128)(2,1)S(1)}, bf16[1,64,1280]{2,1,0:T(8,128)(2,1)S(1)}, u32[]{:S(2)}, u32[]{:S(2)}) collective-permute-start(bf16[1,64,1280]{2,1,0:T(8,128)(2,1)S(1)} %get-tuple-element.244), channel_id=1, source_target_pairs={{1,0},{2,1},{3,2},{4,3},{5,4},{6,5},{7,6},{8,7},{9,8},{10,9},{11,1... | collective-permute-start | bytes 491528 | tf_op jit(solution)/shard_map/ppermute | solution.py:19
  563.9 2.3 copy-start.5
Sparse Core Ops, SparseCore 0:
  11.4 115.0 all-gather.2
  129.3 110.8 all-gather.4
where the time goes:
time: 575 us; the launch traced here: 574 us
  blocking collectives  373 us (65%)
  matrix products  76.8 us (13%)
  local copies, waits for them, and re-layouts  44.2 us (8%)
  waiting for transfers between devices  33.2 us (6%)
  other arithmetic  23.5 us (4%)
  between operations  14.4 us (3%)
  starting transfers between devices  6.94 us (1%)
    psum x2, blocking collectives, group_norm(): totals = lax.psum(jnp.sum(grouped, axis=(0, 2)), 'patch')  193 us
    psum x2, blocking collectives, group_norm(): lax.psum(jnp.sum(jnp.square(grouped - center[None, :, None]), axis=(0, 2)...  179 us
    dynamic_slice x32, local copies, waits for them, and re-layouts, advance(): lax.dynamic_slice_in_dim(value_piece, offset, tok_count, 0)  36.1 us
    all_gather x1, waiting for transfers between devices, shards(): value_piece = lax.all_gather(stale_values, 'patch', axis=0, tiled=True)  28 us
    dot_general x32, matrix products, absorb(): jnp.einsum('qhk,khd->qhd', weights.astype(jnp.bfloat16), value_block, pre...  25.7 us
    dot_general x33, matrix products, scores_of(): jnp.einsum('qhd,khd->qhk', q_heads, key_block, preferred_element_type=jnp...  22.1 us
    dot_general x9, matrix products, shards(): jnp.dot(window, conv_weight[3 * tap_row + tap_col], preferred_element_typ...  19.3 us
    reduce_sum x32, other arithmetic, absorb(): totals = totals * factor + jnp.sum(weights, axis=2)  19.2 us
  transfers between devices with their start and end apart: 4, of which 2 were waited for; matrix products, arithmetic and copies ran while one was open for 3% of the time, Pallas kernels for 0%

commit v1 on v0

v1 whole, which is shorter than its diff:
```python
import functools

import jax
import jax.numpy as jnp
from jax import lax
from jax.experimental import pallas as pl
from jax.experimental.pallas import tpu as pltpu
from jax.sharding import PartitionSpec as P

HEAD = 64
GROUPS = 32
LANES = 128
NY, NZ, NX = 4, 4, 2
EPS = 1e-05
BF = jnp.bfloat16
F32 = jnp.float32
EXACT = lax.Precision.HIGHEST


def shifted(x, dy, dz, dx):
    pairs = []
    for y in range(NY):
        for z in range(NZ):
            for c in range(NX):
                to = (((y + dy) % NY) * NZ + (z + dz) % NZ) * NX + (c + dx) % NX
                pairs.append(((y * NZ + z) * NX + c, to))
    return lax.ppermute(x, "patch", pairs)


def members_of(channels, lead, offset):
    width = channels // GROUPS
    shape = (channels, LANES) if lead else (LANES, channels)
    chan = lax.broadcasted_iota(jnp.int32, shape, 0 if lead else 1)
    group = lax.broadcasted_iota(jnp.int32, shape, 1 if lead else 0) - offset
    inside = (chan >= group * width) & (chan < group * width + width)
    return jnp.where(inside, 1.0, 0.0).astype(F32)


def exact_dot(a, b):
    return jnp.dot(a, b, preferred_element_type=F32, precision=EXACT)


def local_stats(x, peers):
    rows, channels = x.shape
    count = rows * (channels // GROUPS)
    total = jnp.sum(x, axis=0, keepdims=True)
    mean = exact_dot(jnp.broadcast_to(total, (8, channels)), members_of(channels, True, 0)) / count
    center = exact_dot(mean, members_of(channels, False, 0))
    squares = jnp.sum(jnp.square(x - center[:1]), axis=0, keepdims=True)
    spread = exact_dot(
        jnp.broadcast_to(squares, (8, channels)), members_of(channels, True, GROUPS)
    )
    return jnp.broadcast_to((mean + spread)[:1], (peers, LANES))


def combined(stats, channels, count):
    peers = stats.shape[0]
    total = jnp.sum(stats, axis=0, keepdims=True)
    mean = total / peers
    between = jnp.sum(jnp.square(stats - mean), axis=0, keepdims=True) * count
    lead = members_of(channels, False, 0)
    eight = lambda v: jnp.broadcast_to(v, (8, LANES))
    center = exact_dot(eight(mean), lead)[:1]
    spread = exact_dot(eight(between), lead) + exact_dot(
        eight(total), members_of(channels, False, GROUPS)
    )
    return center, lax.rsqrt(spread[:1] / (count * peers) + EPS)


def full(shape):
    return pl.BlockSpec(shape, lambda *_: (0,) * len(shape))


def stats_kernel(x_ref, out_ref):
    out_ref[...] = local_stats(x_ref[...].astype(F32), out_ref.shape[0])


def norm_stats(x, peers):
    return pl.pallas_call(
        stats_kernel,
        out_shape=jax.ShapeDtypeStruct((peers, LANES), F32),
        name="norm_stats",
        cost_estimate=pl.CostEstimate(flops=4 * x.size, bytes_accessed=2 * x.size, transcendentals=0),
    )(x)


def project_kernel(stats_ref, x_ref, gain_ref, wq_ref, wk_ref, wv_ref, q_ref, k_ref, v_ref):
    rows, channels = x_ref.shape
    center, scale = combined(stats_ref[...], channels, rows * (channels // GROUPS))
    normed = ((x_ref[...].astype(F32) - center) * scale * gain_ref[...]).astype(BF)
    for w_ref, o_ref in ((wq_ref, q_ref), (wk_ref, k_ref), (wv_ref, v_ref)):
        o_ref[...] = jnp.dot(normed, w_ref[...], preferred_element_type=F32).astype(BF)


def project(stats, x, gain, wq, wk, wv):
    rows, channels = x.shape
    width = wq.shape[1]
    return pl.pallas_call(
        project_kernel,
        out_shape=[jax.ShapeDtypeStruct((rows, width), BF)] * 3,
        name="project",
        compiler_params=pltpu.CompilerParams(vmem_limit_bytes=24 * 2**20),
        cost_estimate=pl.CostEstimate(
            flops=6 * rows * channels * width,
            bytes_accessed=6 * channels * width,
            transcendentals=0,
        ),
    )(stats, x, gain, wq, wk, wv)


def attend_pair(queries, keys, values):
    rows = queries.shape[0]
    first = lax.broadcasted_iota(jnp.int32, (rows, LANES), 1) < HEAD
    scaled = queries * BF(0.125)
    none = jnp.zeros_like(scaled)
    found = []
    for mine in (jnp.where(first, scaled, none), jnp.where(first, none, scaled)):
        scores = lax.dot_general(
            mine, keys, (((1,), (1,)), ((), ())), preferred_element_type=F32
        )
        top = jnp.max(scores, axis=1, keepdims=True)
        weights = jnp.exp(scores - top).astype(BF)
        both = jnp.dot(weights, values, preferred_element_type=F32)
        found.append((both[:, :LANES], jnp.broadcast_to(top, (rows, LANES)), both[:, LANES:]))
    return first, found


def near_kernel(
    q0, q1, q2, q3, fresh_k, fresh_v, old_k, old_v, a_ref, b_ref, c_ref, sum_ref, top_ref, tot_ref, keys, values
):
    rows = q0.shape[0]
    keys[0:rows, :] = fresh_k[...]
    values[0:rows, 0:LANES] = fresh_v[...]
    for i, ref in enumerate((a_ref, b_ref, c_ref)):
        at = slice((i + 1) * rows, (i + 2) * rows)
        keys[at, :] = ref[0:rows, :]
        values[at, 0:LANES] = ref[rows : 2 * rows, :]
    keys[4 * rows : 5 * rows, :] = old_k[...]
    values[4 * rows : 5 * rows, 0:LANES] = old_v[...]
    values[:, LANES:] = jnp.ones((5 * rows, LANES), BF)
    for band, q_ref in enumerate((q0, q1, q2, q3)):
        span = slice(0, 4 * rows) if band == 0 else slice(rows, 5 * rows)
        first, found = attend_pair(q_ref[...], keys[span, :], values[span, :])
        at = slice(band * rows, (band + 1) * rows)
        for which, out_ref in enumerate((sum_ref, top_ref, tot_ref)):
            out_ref[at, :] = jnp.where(first, found[0][which], found[1][which])


def near_attention(queries, fresh, old, blocks):
    rows, width = queries[0].shape
    pairs = width // LANES
    one = pl.BlockSpec((rows, LANES), lambda j: (0, j))
    two = pl.BlockSpec((2 * rows, LANES), lambda j: (0, j))
    four = pl.BlockSpec((4 * rows, LANES), lambda j: (0, j))
    return pl.pallas_call(
        near_kernel,
        grid=(pairs,),
        in_specs=[one] * 8 + [two] * 3,
        out_specs=[four] * 3,
        out_shape=[jax.ShapeDtypeStruct((4 * rows, width), F32)] * 3,
        scratch_shapes=[pltpu.VMEM((5 * rows, LANES), BF), pltpu.VMEM((5 * rows, 2 * LANES), BF)],
        name="near_attention",
        compiler_params=pltpu.CompilerParams(vmem_limit_bytes=32 * 2**20),
        cost_estimate=pl.CostEstimate(
            flops=64 * rows * rows * width, bytes_accessed=40 * rows * width, transcendentals=0
        ),
    )(*queries, *fresh, *old, *blocks)


def far_kernel(
    q0, q1, q2, q3, a_ref, b_ref, kk_ref, vv_ref, sum_ref, top_ref, tot_ref, o0, o1, o2, o3, keys, values
):
    rows = q0.shape[0]
    j = pl.program_id(0)
    for i, ref in enumerate((a_ref, b_ref)):
        at = slice(i * rows, (i + 1) * rows)
        keys[at, :] = ref[0:rows, :]
        values[at, 0:LANES] = ref[rows : 2 * rows, :]
    keys[2 * rows : 4 * rows, :] = kk_ref[...]
    values[2 * rows : 4 * rows, 0:LANES] = vv_ref[...]
    values[:, LANES:] = jnp.ones((4 * rows, LANES), BF)
    lane = lax.broadcasted_iota(jnp.int32, (rows, LANES), 1)
    width = 5 * LANES
    for band, (q_ref, o_ref) in enumerate(((q0, o0), (q1, o1), (q2, o2), (q3, o3))):
        first, found = attend_pair(q_ref[...], keys[...], values[...])
        at = slice(band * rows, (band + 1) * rows)
        pick = lambda n: jnp.where(first, found[0][n], found[1][n])
        far_top, near_top = pick(1), top_ref[at, :]
        top = jnp.maximum(far_top, near_top)
        far_part, near_part = jnp.exp(far_top - top), jnp.exp(near_top - top)
        total = far_part * pick(2) + near_part * tot_ref[at, :]
        summed = far_part * pick(0) + near_part * sum_ref[at, :]
        o_ref[:, pl.ds(pl.multiple_of(j * LANES, LANES), LANES)] = (summed / total).astype(BF)
        level = top + jnp.log(total)
        swapped = pltpu.roll(level, HEAD, 1)
        row_level = (jnp.where(first, level, swapped), jnp.where(first, swapped, level))
        extra = jnp.where(j == 0, jnp.zeros((rows, LANES), BF), o_ref[:, width:])
        for h in range(2):
            rest = row_level[h]
            for piece in range(3):
                part = rest.astype(BF)
                rest = rest - part.astype(F32)
                extra = jnp.where(lane == 2 * j + h + 10 * piece, part, extra)
        o_ref[:, width:] = extra


def far_attention(queries, blocks, kk, vv, state):
    rows, width = queries[0].shape
    pairs = width // LANES
    one = pl.BlockSpec((rows, LANES), lambda j: (0, j))
    two = pl.BlockSpec((2 * rows, LANES), lambda j: (0, j))
    four = pl.BlockSpec((4 * rows, LANES), lambda j: (0, j))
    wide = width + LANES
    return pl.pallas_call(
        far_kernel,
        grid=(pairs,),
        in_specs=[one] * 4 + [two] * 4 + [four] * 3,
        out_specs=[full((rows, wide))] * 4,
        out_shape=[jax.ShapeDtypeStruct((rows, wide), BF)] * 4,
        scratch_shapes=[pltpu.VMEM((4 * rows, LANES), BF), pltpu.VMEM((4 * rows, 2 * LANES), BF)],
        name="far_attention",
        compiler_params=pltpu.CompilerParams(vmem_limit_bytes=32 * 2**20),
        cost_estimate=pl.CostEstimate(
            flops=64 * rows * rows * width, bytes_accessed=40 * rows * width, transcendentals=0
        ),
    )(*queries, *blocks, kk, vv, *state)


def merge_kernel(p0, p1, p2, p3, x_ref, w_ref, hidden_ref, stats_ref):
    width = w_ref.shape[0]
    lane = lax.broadcasted_iota(jnp.int32, (LANES, width), 0)
    chan = lax.broadcasted_iota(jnp.int32, (LANES, width), 1)
    spread = jnp.zeros((LANES, width), F32)
    for piece in range(3):
        head = lane - 10 * piece
        inside = (head >= 0) & (head < 10) & (chan >= head * HEAD) & (chan < head * HEAD + HEAD)
        spread = jnp.where(inside, 1.0, spread)
    spread = spread.astype(BF)
    parts = (p0, p1, p2, p3)
    levels = [jnp.dot(p[:, width:], spread, preferred_element_type=F32) for p in parts]
    top = functools.reduce(jnp.maximum, levels)
    shares = [jnp.exp(level - top) for level in levels]
    total = functools.reduce(jnp.add, shares)
    summed = functools.reduce(
        jnp.add, [s * p[:, :width].astype(F32) for s, p in zip(shares, parts)]
    )
    attended = (summed / total).astype(BF)
    hidden = x_ref[...].astype(F32) + jnp.dot(attended, w_ref[...], preferred_element_type=F32)
    hidden_ref[...] = hidden
    stats_ref[...] = local_stats(hidden, stats_ref.shape[0])


def merge(parts, x, w_out, peers):
    rows, channels = x.shape
    return pl.pallas_call(
        merge_kernel,
        out_shape=[
            jax.ShapeDtypeStruct((rows, channels), F32),
            jax.ShapeDtypeStruct((peers, LANES), F32),
        ],
        name="merge_project",
        compiler_params=pltpu.CompilerParams(vmem_limit_bytes=24 * 2**20),
        cost_estimate=pl.CostEstimate(
            flops=2 * rows * w_out.size, bytes_accessed=2 * w_out.size, transcendentals=0
        ),
    )(*parts, x, w_out)


def conv_kernel(
    edge_ref, stats_ref, hidden_ref, above_ref, below_ref, gain_ref, w_ref, shift_ref, out_ref, moved, total, cols
):
    tap = pl.program_id(0)
    rows, channels = hidden_ref.shape
    width = out_ref.shape[1]

    @pl.when(tap == 0)
    def _():
        center, scale = combined(stats_ref[...], channels, rows * (channels // GROUPS))
        pieces = (
            (above_ref, 0, cols, edge_ref[0] == 0),
            (hidden_ref, cols, rows, None),
            (below_ref, cols + rows, cols, edge_ref[1] == 0),
        )
        for ref, start, size, kept in pieces:
            for part in range(size // cols):
                at = slice(part * cols, (part + 1) * cols)
                v = (ref[at, :] - center) * scale * gain_ref[...]
                v = v / (1.0 + jnp.exp(-v))
                if kept is not None:
                    v = jnp.where(kept, v, 0.0)
                col = lax.broadcasted_iota(jnp.int32, (cols, channels), 0)
                to = slice(start + part * cols, start + (part + 1) * cols)
                moved[1, to, :] = v.astype(BF)
                moved[0, to, :] = jnp.where(col == 0, 0.0, pltpu.roll(v, 1, 0)).astype(BF)
                moved[2, to, :] = jnp.where(col == cols - 1, 0.0, pltpu.roll(v, cols - 1, 0)).astype(BF)
        total[...] = hidden_ref[:, :width] + shift_ref[...]

    row = lax.div(tap, 3)
    window = moved[lax.rem(tap, 3), pl.ds(pl.multiple_of(row * cols, cols), rows), :]
    total[...] += jnp.dot(window, w_ref[0], preferred_element_type=F32)

    @pl.when(tap == pl.num_programs(0) - 1)
    def _():
        out_ref[...] = total[...].astype(BF)


def convolve(edges, stats, hidden, above, below, gain, weight, shift):
    rows, channels = hidden.shape
    cols = above.shape[0]
    width = weight.shape[2]
    return pl.pallas_call(
        functools.partial(conv_kernel, cols=cols),
        grid=(9,),
        in_specs=[
            pl.BlockSpec(memory_space=pltpu.SMEM),
            full(stats.shape),
            full(hidden.shape),
            full(above.shape),
            full(below.shape),
            full(gain.shape),
            pl.BlockSpec((1, channels, width), lambda t: (t, 0, 0)),
            full(shift.shape),
        ],
        out_specs=full((rows, width)),
        out_shape=jax.ShapeDtypeStruct((rows, width), BF),
        scratch_shapes=[
            pltpu.VMEM((3, rows + 2 * cols, channels), BF),
            pltpu.VMEM((rows, width), F32),
        ],
        name="norm_convolve",
        compiler_params=pltpu.CompilerParams(vmem_limit_bytes=32 * 2**20),
        cost_estimate=pl.CostEstimate(
            flops=2 * rows * weight.size, bytes_accessed=2 * weight.size, transcendentals=0
        ),
    )(edges, stats, hidden, above, below, gain, weight, shift)


def everyones(stats):
    return lax.all_to_all(stats, "patch", 0, 0, tiled=True)


def shards(
    latent,
    gn_gain,
    w_query,
    w_key,
    w_value,
    w_out,
    stale_keys,
    stale_values,
    gn2_gain,
    conv_weight,
    time_shift,
):
    row_count, col_count, channels = latent.shape
    tok_count = row_count * col_count
    peers = lax.axis_size("patch")
    own = lax.axis_index("patch")
    x = latent.reshape(tok_count, channels)
    old = jnp.concatenate([stale_keys, stale_values], axis=0)
    from_below = shifted(old, 1, 0, 0)
    from_above = shifted(old, -1, 0, 0)
    from_side = shifted(old, 0, 0, 1)

    stats = everyones(norm_stats(x, peers))
    queries, fresh_keys, fresh_values = project(
        stats, x, gn_gain.reshape(1, channels), w_query, w_key, w_value
    )
    side_below = shifted(from_side, 1, 0, 0)
    side_above = shifted(from_side, -1, 0, 0)
    bands = (
        queries,
        shifted(queries, 0, 1, 0),
        shifted(queries, 0, -1, 0),
        shifted(queries, 0, 2, 0),
    )
    last_keys = shifted(jnp.concatenate([from_below[:tok_count], side_below[:tok_count]]), 1, 0, 0)
    last_values = shifted(jnp.concatenate([from_above[tok_count:], side_above[tok_count:]]), -1, 0, 0)

    state = near_attention(
        bands,
        (fresh_keys, fresh_values),
        (stale_keys, stale_values),
        (from_below, from_above, from_side),
    )
    parts = far_attention(bands, (side_below, side_above), last_keys, last_values, state)
    parts = (
        parts[0],
        shifted(parts[1], 0, -1, 0),
        shifted(parts[2], 0, 1, 0),
        shifted(parts[3], 0, 2, 0),
    )
    hidden, stats = merge(parts, x, w_out, peers)
    down = [(i, i + 1) for i in range(peers - 1)]
    above = lax.ppermute(hidden[tok_count - col_count :], "patch", down)
    below = lax.ppermute(hidden[:col_count], "patch", [(j, i) for i, j in down])
    edges = jnp.stack([own == 0, own == peers - 1]).astype(jnp.int32)
    result = convolve(
        edges,
        everyones(stats),
        hidden,
        above,
        below,
        gn2_gain.reshape(1, channels),
        conv_weight,
        time_shift.reshape(1, -1),
    )
    return (result.reshape(row_count, col_count, -1), fresh_keys, fresh_values)


def solution(mesh):
    placed = (
        P(("batch", "patch"), None, None),
        P(),
        P(),
        P(),
        P(),
        P(),
        P(("batch", "patch"), None),
        P(("batch", "patch"), None),
        P(),
        P(),
        P("batch"),
    )
    return jax.shard_map(
        shards,
        mesh=mesh,
        in_specs=placed,
        out_specs=(
            P(("batch", "patch"), None, None),
            P(("batch", "patch"), None),
            P(("batch", "patch"), None),
        ),
        check_vma=False,
    )
```

time: 575 us -> 165 us (0.29)
  blocking collectives: 373 us -> 0 us
  matrix products: 76.8 us -> 0 us
  Pallas kernels: 0 us -> 55.5 us
  starting transfers between devices: 6.94 us -> 43.7 us
  local copies, waits for them, and re-layouts: 44.2 us -> 13.4 us
  other arithmetic: 23.5 us -> 1.86 us
  waiting for transfers between devices: 33.2 us -> 49.2 us
  between operations: 14.4 us -> 0.9 us
    psum x4 -> x0, blocking collectives: 373 us -> none  [the longest x2 193 us: group_norm(): totals = lax.psum(jnp.sum(grouped, axis=(0, 2)), 'patch')]
    dot_general x79 -> x0, matrix products: 76.8 us -> none  [the longest x32 25.7 us: absorb(): jnp.einsum('qhk,khd->qhd', weights.astype(jnp.bfloat16), value_block, pre...]
    pallas_call x0 -> x6, Pallas kernels: none -> 55.5 us  [the longest x1 18.4 us: far_attention(): pl.pallas_call(far_kernel, grid=(pairs,), in_specs=[one] * 4 + [two] * 4...]
    dynamic_slice x32 -> x0, local copies, waits for them, and re-layouts: 36.1 us -> none  [advance(): lax.dynamic_slice_in_dim(value_piece, offset, tok_count, 0)]
    ppermute x2 -> x15, waiting for transfers between devices: 5.09 us -> 37.4 us  [the longest x13 37.4 us: shifted(): return lax.ppermute(x, 'patch', pairs)]
    all_gather x2 -> x0, waiting for transfers between devices: 28 us -> none  [the longest x1 28 us: shards(): value_piece = lax.all_gather(stale_values, 'patch', axis=0, tiled=True)]
    reduce_sum x40 -> x0, other arithmetic: 20.6 us -> none  [the longest x32 19.2 us: absorb(): totals = totals * factor + jnp.sum(weights, axis=2)]
    ppermute x2 -> x15, starting transfers between devices: 6.86 us -> 26.8 us  [the longest x13 20.5 us: shifted(): return lax.ppermute(x, 'patch', pairs)]
  transfers between devices with their start and end apart: 4 -> 17, of which waited for: 2 -> 7; matrix products, arithmetic and copies ran while one was open for 3% -> 2% of each run, Pallas kernels for 0% -> 14%
where the time goes in v1:
time: 165 us
  Pallas kernels  55.5 us (34%)
  waiting for transfers between devices  49.2 us (30%)
  starting transfers between devices  43.7 us (26%)
  local copies, waits for them, and re-layouts  13.4 us (8%)
  other arithmetic  1.86 us (1%)
    ppermute x13, waiting for transfers between devices, shifted(): return lax.ppermute(x, 'patch', pairs)  37.4 us
    ppermute x13, starting transfers between devices, shifted(): return lax.ppermute(x, 'patch', pairs)  20.5 us
    pallas_call x1, Pallas kernels, far_attention(): pl.pallas_call(far_kernel, grid=(pairs,), in_specs=[one] * 4 + [two] * 4...  18.4 us
    pallas_call x1, Pallas kernels, near_attention(): pl.pallas_call(near_kernel, grid=(pairs,), in_specs=[one] * 8 + [two] * 3...  16.9 us
    all_to_all x2, starting transfers between devices, everyones(): return lax.all_to_all(stats, 'patch', 0, 0, tiled=True)  16.9 us
    all_to_all x2, waiting for transfers between devices, everyones(): return lax.all_to_all(stats, 'patch', 0, 0, tiled=True)  11.8 us
    unnamed x35, local copies, waits for them, and re-layouts  11.2 us
    pallas_call x1, Pallas kernels, convolve(): pl.pallas_call(functools.partial(conv_kernel, cols=cols), grid=(9,), in_s...  9.82 us
  transfers between devices with their start and end apart: 17, of which 7 were waited for; matrix products, arithmetic and copies ran while one was open for 2% of the time, Pallas kernels for 14%

profile of v1, /device:TPU:0, one launch (start us, length us, event | category | flops | bytes accessed | tf_op | source)
XLA Modules:
  0.0 164.6 jit_solution(3646401645642659618)
XLA Ops:
  0.6 1.0 constant_dynamic-update-slice_fusion.1
  1.6 1.0 constant_dynamic-update-slice_fusion
  2.7 3.2 %collective-permute-start.3 = (bf16[512,640]{1,0:T(8,128)(2,1)S(1)}, bf16[512,640]{1,0:T(8,128)(2,1)}, u32[]{:S(2)}, u32[]{:S(2)}) collective-permute-start(bf16[512,640]{1,0:T(8,128)(2,1)S(1)} %constant_dynamic-update-slice_fusion), channel_id=1, source_target_pairs={{0,1},{1,0},{2,3},{3,2},{4,5},{5,4},{6,7},{7,6},{8,9},{9,8},{10,11... | collective-permute-start | bytes 1966088 | tf_op jit(solution)/shard_map/ppermute | solution.py:27
  5.9 1.6 collective-permute-start.6
  7.4 1.7 %collective-permute-start.8 = (bf16[512,640]{1,0:T(8,128)(2,1)S(1)}, bf16[512,640]{1,0:T(8,128)(2,1)S(1)}, u32[]{:S(2)}, u32[]{:S(2)}) collective-permute-start(bf16[512,640]{1,0:T(8,128)(2,1)S(1)} %constant_dynamic-update-slice_fusion), channel_id=1, source_target_pairs={{0,24},{1,25},{2,26},{3,27},{4,28},{5,29},{6,30},{7,31},{8,0},{9,1... | collective-permute-start | bytes 1966088 | tf_op jit(solution)/shard_map/ppermute | solution.py:27
  9.1 11.6 %collective-permute-done.3.c_ref = bf16[512,640]{1,0:T(8,128)(2,1)} collective-permute-done((bf16[512,640]{1,0:T(8,128)(2,1)S(1)}, bf16[512,640]{1,0:T(8,128)(2,1)}, u32[]{:S(2)}, u32[]{:S(2)}) %collective-permute-start.3) | collective-permute-done | bytes 655392 | tf_op jit(solution)/shard_map/ppermute | solution.py:27
  20.7 1.8 %collective-permute-start.4 = (bf16[512,640]{1,0:T(8,128)(2,1)}, bf16[512,640]{1,0:T(8,128)(2,1)S(1)}, u32[]{:S(2)}, u32[]{:S(2)}) collective-permute-start(bf16[512,640]{1,0:T(8,128)(2,1)} %collective-permute-done.3.c_ref), channel_id=1, source_target_pairs={{0,8},{1,9},{2,10},{3,11},{4,12},{5,13},{6,14},{7,15},{8,16},{9,17... | collective-permute-start | bytes 1966088 | tf_op jit(solution)/shard_map/ppermute | solution.py:27
  22.5 1.4 collective-permute-start.5
  23.9 3.3 %norm_stats.1 = f32[32,128]{1,0:T(8,128)} custom-call(bf16[256,1280]{1,0:T(8,128)(2,1)} %bitcast.12), custom_call_target="tpu_custom_call" | custom-call | flops 1310720 | bytes 655360 | tf_op jit(solution)/shard_map/norm_stats/pallas_call | solution.py:79
  27.3 9.8 %all-to-all-start = ((f32[32,1,128]{2,1,0:T(1,128)}), f32[32,1,128]{2,1,0:T(1,128)S(1)}, u32[]{:S(2)}, u32[]{:S(2)}) async-start(f32[32,1,128]{2,1,0:T(1,128)} %bitcast.18), calls=%async_computation | async-start | bytes 32768 | tf_op jit(solution)/shard_map/all_to_all | solution.py:339
  37.2 0.8 collective-permute-done.4.a_ref
  38.0 0.2 copy-done.10
  38.2 0.0 copy-start.1
  38.2 0.0 copy-start.3
  38.2 0.9 pad_maximum_fusion
  39.1 1.8 %collective-permute-start.7 = (bf16[512,640]{1,0:T(8,128)(2,1)}, bf16[512,640]{1,0:T(8,128)(2,1)}, u32[]{:S(2)}, u32[]{:S(2)}) collective-permute-start(bf16[512,640]{1,0:T(8,128)(2,1)} %pad_maximum_fusion), channel_id=1, source_target_pairs={{0,8},{1,9},{2,10},{3,11},{4,12},{5,13},{6,14},{7,15},{8,16},{9,17... | collective-permute-start | bytes 1966088 | tf_op jit(solution)/shard_map/ppermute | solution.py:27
  40.9 0.0 collective-permute-done.5.b_ref
  40.9 1.0 slice.27
  41.9 0.9 pad_maximum_fusion.1
  42.8 1.4 collective-permute-start.9
  44.3 2.5 %all-to-all-done = f32[32,1,128]{2,1,0:T(1,128)S(1)} async-done(((f32[32,1,128]{2,1,0:T(1,128)}), f32[32,1,128]{2,1,0:T(1,128)S(1)}, u32[]{:S(2)}, u32[]{:S(2)}) %all-to-all-start) | async-done | bytes 16416 | tf_op jit(solution)/shard_map/all_to_all | solution.py:339
  46.7 1.4 copy-done.4
  48.2 1.4 copy-done.5
  49.6 3.5 %project.1 = (bf16[256,640]{1,0:T(8,128)(2,1)S(1)}, bf16[256,640]{1,0:T(8,128)(2,1)}, bf16[256,640]{1,0:T(8,128)(2,1)}) custom-call(f32[32,128]{1,0:T(8,128)S(1)} %bitcast.15, bf16[256,1280]{1,0:T(8,128)(2,1)S(1)} %bitcast.13, f32[1,1280]{1,0:T(1,128)S(1)} %reshape.26.gain_ref, bf16[1280,640]{1,0:T(8,128)(2,1)S(1)} %copy-done.3, ...), custom_call_target="tpu_custom_call" | custom-call | flops 1258291200 | bytes 4915200 | tf_op jit(solution)/shard_map/project/pallas_call | solution.py:98
  53.1 0.6 collective-permute-start
  53.7 2.7 %collective-permute-start.1 = (bf16[256,640]{1,0:T(8,128)(2,1)S(1)}, bf16[256,640]{1,0:T(8,128)(2,1)S(1)}, u32[]{:S(2)}, u32[]{:S(2)}) collective-permute-start(bf16[256,640]{1,0:T(8,128)(2,1)S(1)} %get-tuple-element.15.q0), channel_id=1, source_target_pairs={{0,6},{1,7},{2,0},{3,1},{4,2},{5,3},{6,4},{7,5},{8,14},{9,15},{10,... | collective-permute-start | bytes 983048 | tf_op jit(solution)/shard_map/ppermute | solution.py:27
  56.3 0.1 collective-permute-start.2
  56.5 11.8 %collective-permute-done.q1 = bf16[256,640]{1,0:T(8,128)(2,1)S(1)} collective-permute-done((bf16[256,640]{1,0:T(8,128)(2,1)S(1)}, bf16[256,640]{1,0:T(8,128)(2,1)S(1)}, u32[]{:S(2)}, u32[]{:S(2)}) %collective-permute-start) | collective-permute-done | bytes 327712 | tf_op jit(solution)/shard_map/ppermute | solution.py:27
  68.3 0.0 copy-start.12
  68.3 1.0 copy-done.12
  69.3 1.0 copy-done.13
  70.2 16.9 %near_attention.1 = (f32[1024,640]{1,0:T(8,128)S(1)}, f32[1024,640]{1,0:T(8,128)S(1)}, f32[1024,640]{1,0:T(8,128)S(1)}) custom-call(bf16[256,640]{1,0:T(8,128)(2,1)S(1)} %get-tuple-element.15.q0, bf16[256,640]{1,0:T(8,128)(2,1)S(1)} %collective-permute-done.q1, bf16[256,640]{1,0:T(8,128)(2,1)S(1)} %collective-permute-done.1.q2, ...), custom_call_target="tpu_custom_call" | custom-call | flops 2684354560 | bytes 6553600 | tf_op jit(solution)/shard_map/near_attention/pallas_call | solution.py:155
  87.1 0.0 collective-permute-done.9.vv_ref
  87.1 0.0 copy-start.2
  87.2 18.4 %far_attention.1 = (bf16[256,768]{1,0:T(8,128)(2,1)S(1)}, bf16[256,768]{1,0:T(8,128)(2,1)S(1)}, bf16[256,768]{1,0:T(8,128)(2,1)S(1)}, bf16[256,768]{1,0:T(8,128)(2,1)S(1)}) custom-call(bf16[256,640]{1,0:T(8,128)(2,1)S(1)} %get-tuple-element.15.q0, bf16[256,640]{1,0:T(8,128)(2,1)S(1)} %collective-permute-done.q1, ...), custom_call_target="tpu_custom_call" | custom-call | flops 2684354560 | bytes 6553600 | tf_op jit(solution)/shard_map/far_attention/pallas_call | solution.py:214
  105.6 2.7 %collective-permute-start.10 = (bf16[256,768]{1,0:T(8,128)(2,1)S(1)}, bf16[256,768]{1,0:T(8,128)(2,1)S(1)}, u32[]{:S(2)}, u32[]{:S(2)}) collective-permute-start(bf16[256,768]{1,0:T(8,128)(2,1)S(1)} %get-tuple-element.22), channel_id=1, source_target_pairs={{0,6},{1,7},{2,0},{3,1},{4,2},{5,3},{6,4},{7,5},{8,14},{9,15},{10,... | collective-permute-start | bytes 1179656 | tf_op jit(solution)/shard_map/ppermute | solution.py:27
  108.3 1.5 collective-permute-start.12
  109.8 11.0 %collective-permute-done.10.p1 = bf16[256,768]{1,0:T(8,128)(2,1)S(1)} collective-permute-done((bf16[256,768]{1,0:T(8,128)(2,1)S(1)}, bf16[256,768]{1,0:T(8,128)(2,1)S(1)}, u32[]{:S(2)}, u32[]{:S(2)}) %collective-permute-start.10) | collective-permute-done | bytes 393248 | tf_op jit(solution)/shard_map/ppermute | solution.py:27
  120.8 2.2 %collective-permute-done.11.p2 = bf16[256,768]{1,0:T(8,128)(2,1)S(1)} collective-permute-done((bf16[256,768]{1,0:T(8,128)(2,1)S(1)}, bf16[256,768]{1,0:T(8,128)(2,1)S(1)}, u32[]{:S(2)}, u32[]{:S(2)}) %collective-permute-start.11) | collective-permute-done | bytes 393248 | tf_op jit(solution)/shard_map/ppermute | solution.py:27
  123.0 0.0 copy-start.16
  123.0 3.6 %merge_project.1 = (f32[256,1280]{1,0:T(8,128)S(1)}, f32[32,128]{1,0:T(8,128)}) custom-call(bf16[256,768]{1,0:T(8,128)(2,1)S(1)} %get-tuple-element.21.p0, bf16[256,768]{1,0:T(8,128)(2,1)S(1)} %collective-permute-done.10.p1, bf16[256,768]{1,0:T(8,128)(2,1)S(1)} %collective-permute-done.11.p2, bf16[256,768]{1,0:T(8,128)(2,1)S(1)} %collective-permute-done.12.p3, ...), custom_call_target="tpu_custom_call" | custom-call | flops 419430400 | bytes 1638400 | tf_op jit(solution)/shard_map/merge_project/pallas_call | solution.py:255
  126.6 5.1 %collective-permute-start.13 = (f32[64,1280]{1,0:T(8,128)S(1)}, f32[64,1280]{1,0:T(8,128)S(1)}, u32[]{:S(2)}, u32[]{:S(2)}) collective-permute-start(f32[64,1280]{1,0:T(8,128)S(1)} %get-tuple-element.28), channel_id=1, source_target_pairs={{0,1},{1,2},{2,3},{3,4},{4,5},{5,6},{6,7},{7,8},{8,9},{9,10},{10,1... | collective-permute-start | bytes 983048 | tf_op jit(solution)/shard_map/ppermute | solution.py:395
  131.7 1.3 collective-permute-start.14
  133.0 7.1 %all-to-all-start.1 = ((f32[32,1,128]{2,1,0:T(1,128)}), f32[32,1,128]{2,1,0:T(1,128)S(1)}, u32[]{:S(2)}, u32[]{:S(2)}) async-start(f32[32,1,128]{2,1,0:T(1,128)} %bitcast.7), calls=%async_computation.1 | async-start | bytes 32768 | tf_op jit(solution)/shard_map/all_to_all | solution.py:339
  140.1 0.1 add_convert_fusion.edge_ref
  140.2 9.3 %all-to-all-done.1 = f32[32,1,128]{2,1,0:T(1,128)S(1)} async-done(((f32[32,1,128]{2,1,0:T(1,128)}), f32[32,1,128]{2,1,0:T(1,128)S(1)}, u32[]{:S(2)}, u32[]{:S(2)}) %all-to-all-start.1) | async-done | bytes 16416 | tf_op jit(solution)/shard_map/all_to_all | solution.py:339
  149.5 5.2 %copy-done = bf16[9,1280,640]{2,1,0:T(8,128)(2,1)S(1)} copy-done((bf16[9,1280,640]{2,1,0:T(8,128)(2,1)S(1)}, bf16[9,1280,640]{2,1,0:T(8,128)(2,1)}, u32[]{:S(2)}) %copy-start) | copy-done | bytes 14745624
  154.7 9.8 %norm_convolve.1 = bf16[256,640]{1,0:T(8,128)(2,1)} custom-call(s32[2]{0:T(128)S(1)} %add_convert_fusion.edge_ref, f32[32,128]{1,0:T(8,128)S(1)} %bitcast.16, f32[256,1280]{1,0:T(8,128)S(1)} %get-tuple-element.26.hidden_ref, f32[64,1280]{1,0:T(8,128)S(1)} %collective-permute-done.13.above_ref, f32[64,1280]{1,0:T(8,128)S(1)} %collective-permute-done.14.below_ref, ...), custom_call_target="tpu_custom_call" | custom-call | flops 3774873600 | bytes 14745600 | tf_op jit(solution)/shard_map/norm_convolve/pallas_call | solution.py:311
  (39 shorter events, 0.2 us)
Async XLA Ops:
  0.6 36.4 %copy-start.14 = (f32[1280]{0:T(1024)S(1)}, f32[1280]{0:T(1024)}, u32[]{:S(2)}) copy-start(f32[1280]{0:T(1024)} %param.12) | copy-start | bytes 15364
  2.7 18.0 %collective-permute-start.3 = (bf16[512,640]{1,0:T(8,128)(2,1)S(1)}, bf16[512,640]{1,0:T(8,128)(2,1)}, u32[]{:S(2)}, u32[]{:S(2)}) collective-permute-start(bf16[512,640]{1,0:T(8,128)(2,1)S(1)} %constant_dynamic-update-slice_fusion), channel_id=1, source_target_pairs={{0,1},{1,0},{2,3},{3,2},{4,5},{5,4},{6,7},{7,6},{8,9},{9,8},{10,11... | collective-permute-start | bytes 1966088 | tf_op jit(solution)/shard_map/ppermute | solution.py:27
  5.9 31.2 %collective-permute-start.6 = (bf16[512,640]{1,0:T(8,128)(2,1)S(1)}, bf16[512,640]{1,0:T(8,128)(2,1)S(1)}, u32[]{:S(2)}, u32[]{:S(2)}) collective-permute-start(bf16[512,640]{1,0:T(8,128)(2,1)S(1)} %constant_dynamic-update-slice_fusion), channel_id=1, source_target_pairs={{0,8},{1,9},{2,10},{3,11},{4,12},{5,13},{6,14},{7,15},{8,16},{9,17... | collective-permute-start | bytes 1966088 | tf_op jit(solution)/shard_map/ppermute | solution.py:27
  7.4 29.7 %collective-permute-start.8 = (bf16[512,640]{1,0:T(8,128)(2,1)S(1)}, bf16[512,640]{1,0:T(8,128)(2,1)S(1)}, u32[]{:S(2)}, u32[]{:S(2)}) collective-permute-start(bf16[512,640]{1,0:T(8,128)(2,1)S(1)} %constant_dynamic-update-slice_fusion), channel_id=1, source_target_pairs={{0,24},{1,25},{2,26},{3,27},{4,28},{5,29},{6,30},{7,31},{8,0},{9,1... | collective-permute-start | bytes 1966088 | tf_op jit(solution)/shard_map/ppermute | solution.py:27
  20.7 17.3 %collective-permute-start.4 = (bf16[512,640]{1,0:T(8,128)(2,1)}, bf16[512,640]{1,0:T(8,128)(2,1)S(1)}, u32[]{:S(2)}, u32[]{:S(2)}) collective-permute-start(bf16[512,640]{1,0:T(8,128)(2,1)} %collective-permute-done.3.c_ref), channel_id=1, source_target_pairs={{0,8},{1,9},{2,10},{3,11},{4,12},{5,13},{6,14},{7,15},{8,16},{9,17... | collective-permute-start | bytes 1966088 | tf_op jit(solution)/shard_map/ppermute | solution.py:27
  22.5 18.4 %collective-permute-start.5 = (bf16[512,640]{1,0:T(8,128)(2,1)}, bf16[512,640]{1,0:T(8,128)(2,1)}, u32[]{:S(2)}, u32[]{:S(2)}) collective-permute-start(bf16[512,640]{1,0:T(8,128)(2,1)} %collective-permute-done.3.c_ref), channel_id=1, source_target_pairs={{0,24},{1,25},{2,26},{3,27},{4,28},{5,29},{6,30},{7,31},{8,0},{9,1... | collective-permute-start | bytes 1966088 | tf_op jit(solution)/shard_map/ppermute | solution.py:27
  27.3 19.5 %all-to-all-start = ((f32[32,1,128]{2,1,0:T(1,128)}), f32[32,1,128]{2,1,0:T(1,128)S(1)}, u32[]{:S(2)}, u32[]{:S(2)}) async-start(f32[32,1,128]{2,1,0:T(1,128)} %bitcast.18), calls=%async_computation | async-start | bytes 32768 | tf_op jit(solution)/shard_map/all_to_all | solution.py:339
  37.1 0.9 copy-start.8
  37.2 1.0 copy-start.10
  38.2 8.5 %copy-start.1 = (bf16[4,64,1280]{2,1,0:T(8,128)(2,1)S(1)}, bf16[4,64,1280]{2,1,0:T(8,128)(2,1)}, u32[]{:S(2)}) copy-start(bf16[4,64,1280]{2,1,0:T(8,128)(2,1)} %param.11) | copy-start | bytes 1966084
  38.2 8.5 %copy-start.3 = (bf16[1280,640]{1,0:T(8,128)(2,1)S(1)}, bf16[1280,640]{1,0:T(8,128)(2,1)}, u32[]{:S(2)}) copy-start(bf16[1280,640]{1,0:T(8,128)(2,1)} %wq_ref.1) | copy-start | bytes 4915204
  39.1 48.0 %collective-permute-start.7 = (bf16[512,640]{1,0:T(8,128)(2,1)}, bf16[512,640]{1,0:T(8,128)(2,1)}, u32[]{:S(2)}, u32[]{:S(2)}) collective-permute-start(bf16[512,640]{1,0:T(8,128)(2,1)} %pad_maximum_fusion), channel_id=1, source_target_pairs={{0,8},{1,9},{2,10},{3,11},{4,12},{5,13},{6,14},{7,15},{8,16},{9,17... | collective-permute-start | bytes 1966088 | tf_op jit(solution)/shard_map/ppermute | solution.py:27
  42.8 44.3 %collective-permute-start.9 = (bf16[512,640]{1,0:T(8,128)(2,1)}, bf16[512,640]{1,0:T(8,128)(2,1)}, u32[]{:S(2)}, u32[]{:S(2)}) collective-permute-start(bf16[512,640]{1,0:T(8,128)(2,1)} %pad_maximum_fusion.1), channel_id=1, source_target_pairs={{0,24},{1,25},{2,26},{3,27},{4,28},{5,29},{6,30},{7,31},{8,0},{9,1... | collective-permute-start | bytes 1966088 | tf_op jit(solution)/shard_map/ppermute | solution.py:27
  46.7 1.4 copy-start.4
  48.2 1.4 copy-start.5
  49.6 18.6 %copy-start.6 = (bf16[256,640]{1,0:T(8,128)(2,1)S(1)}, bf16[256,640]{1,0:T(8,128)(2,1)}, u32[]{:S(2)}) copy-start(bf16[256,640]{1,0:T(8,128)(2,1)} %old_k.1) | copy-start | bytes 983044
  49.6 18.6 %copy-start.7 = (bf16[256,640]{1,0:T(8,128)(2,1)S(1)}, bf16[256,640]{1,0:T(8,128)(2,1)}, u32[]{:S(2)}) copy-start(bf16[256,640]{1,0:T(8,128)(2,1)} %old_v.1) | copy-start | bytes 983044
  49.6 18.7 %copy-start.9 = (bf16[512,640]{1,0:T(8,128)(2,1)S(1)}, bf16[512,640]{1,0:T(8,128)(2,1)}, u32[]{:S(2)}) copy-start(bf16[512,640]{1,0:T(8,128)(2,1)} %copy-done.8) | copy-start | bytes 1966084
  49.6 18.7 %copy-start.11 = (bf16[512,640]{1,0:T(8,128)(2,1)S(1)}, bf16[512,640]{1,0:T(8,128)(2,1)}, u32[]{:S(2)}) copy-start(bf16[512,640]{1,0:T(8,128)(2,1)} %copy-done.10) | copy-start | bytes 1966084
  53.1 15.1 %collective-permute-start = (bf16[256,640]{1,0:T(8,128)(2,1)S(1)}, bf16[256,640]{1,0:T(8,128)(2,1)S(1)}, u32[]{:S(2)}, u32[]{:S(2)}) collective-permute-start(bf16[256,640]{1,0:T(8,128)(2,1)S(1)} %get-tuple-element.15.q0), channel_id=1, source_target_pairs={{0,2},{1,3},{2,4},{3,5},{4,6},{5,7},{6,0},{7,1},{8,10},{9,11},{10,... | collective-permute-start | bytes 983048 | tf_op jit(solution)/shard_map/ppermute | solution.py:27
  53.7 14.6 %collective-permute-start.1 = (bf16[256,640]{1,0:T(8,128)(2,1)S(1)}, bf16[256,640]{1,0:T(8,128)(2,1)S(1)}, u32[]{:S(2)}, u32[]{:S(2)}) collective-permute-start(bf16[256,640]{1,0:T(8,128)(2,1)S(1)} %get-tuple-element.15.q0), channel_id=1, source_target_pairs={{0,6},{1,7},{2,0},{3,1},{4,2},{5,3},{6,4},{7,5},{8,14},{9,15},{10,... | collective-permute-start | bytes 983048 | tf_op jit(solution)/shard_map/ppermute | solution.py:27
  56.3 11.9 %collective-permute-start.2 = (bf16[256,640]{1,0:T(8,128)(2,1)S(1)}, bf16[256,640]{1,0:T(8,128)(2,1)S(1)}, u32[]{:S(2)}, u32[]{:S(2)}) collective-permute-start(bf16[256,640]{1,0:T(8,128)(2,1)S(1)} %get-tuple-element.15.q0), channel_id=1, source_target_pairs={{0,4},{1,5},{2,6},{3,7},{4,0},{5,1},{6,2},{7,3},{8,12},{9,13},{10,... | collective-permute-start | bytes 983048 | tf_op jit(solution)/shard_map/ppermute | solution.py:27
  68.3 1.0 copy-start.12
  69.3 1.0 copy-start.13
  87.1 35.8 %copy-start.2 = (bf16[640,1280]{1,0:T(8,128)(2,1)S(1)}, bf16[640,1280]{1,0:T(8,128)(2,1)}, u32[]{:S(2)}) copy-start(bf16[640,1280]{1,0:T(8,128)(2,1)} %w_ref.2) | copy-start | bytes 4915204
  105.6 15.2 %collective-permute-start.10 = (bf16[256,768]{1,0:T(8,128)(2,1)S(1)}, bf16[256,768]{1,0:T(8,128)(2,1)S(1)}, u32[]{:S(2)}, u32[]{:S(2)}) collective-permute-start(bf16[256,768]{1,0:T(8,128)(2,1)S(1)} %get-tuple-element.22), channel_id=1, source_target_pairs={{0,6},{1,7},{2,0},{3,1},{4,2},{5,3},{6,4},{7,5},{8,14},{9,15},{10,... | collective-permute-start | bytes 1179656 | tf_op jit(solution)/shard_map/ppermute | solution.py:27
  108.3 14.7 %collective-permute-start.11 = (bf16[256,768]{1,0:T(8,128)(2,1)S(1)}, bf16[256,768]{1,0:T(8,128)(2,1)S(1)}, u32[]{:S(2)}, u32[]{:S(2)}) collective-permute-start(bf16[256,768]{1,0:T(8,128)(2,1)S(1)} %get-tuple-element.23), channel_id=1, source_target_pairs={{0,2},{1,3},{2,4},{3,5},{4,6},{5,7},{6,0},{7,1},{8,10},{9,11},{10,... | collective-permute-start | bytes 1179656 | tf_op jit(solution)/shard_map/ppermute | solution.py:27
  108.3 14.7 %collective-permute-start.12 = (bf16[256,768]{1,0:T(8,128)(2,1)S(1)}, bf16[256,768]{1,0:T(8,128)(2,1)S(1)}, u32[]{:S(2)}, u32[]{:S(2)}) collective-permute-start(bf16[256,768]{1,0:T(8,128)(2,1)S(1)} %get-tuple-element.24), channel_id=1, source_target_pairs={{0,4},{1,5},{2,6},{3,7},{4,0},{5,1},{6,2},{7,3},{8,12},{9,13},{10,... | collective-permute-start | bytes 1179656 | tf_op jit(solution)/shard_map/ppermute | solution.py:27
  123.0 17.2 %copy-start.15 = (f32[1280]{0:T(1024)S(1)}, f32[1280]{0:T(1024)}, u32[]{:S(2)}) copy-start(f32[1280]{0:T(1024)} %param.19) | copy-start | bytes 15364
  123.0 17.2 %copy-start.16 = (f32[640]{0:T(1024)S(1)}, f32[640]{0:T(1024)}, u32[]{:S(2)}) copy-start(f32[640]{0:T(1024)} %param.21) | copy-start | bytes 7684
  126.6 22.9 %collective-permute-start.13 = (f32[64,1280]{1,0:T(8,128)S(1)}, f32[64,1280]{1,0:T(8,128)S(1)}, u32[]{:S(2)}, u32[]{:S(2)}) collective-permute-start(f32[64,1280]{1,0:T(8,128)S(1)} %get-tuple-element.28), channel_id=1, source_target_pairs={{0,1},{1,2},{2,3},{3,4},{4,5},{5,6},{6,7},{7,8},{8,9},{9,10},{10,1... | collective-permute-start | bytes 983048 | tf_op jit(solution)/shard_map/ppermute | solution.py:395
  131.7 17.8 %collective-permute-start.14 = (f32[64,1280]{1,0:T(8,128)S(1)}, f32[64,1280]{1,0:T(8,128)S(1)}, u32[]{:S(2)}, u32[]{:S(2)}) collective-permute-start(f32[64,1280]{1,0:T(8,128)S(1)} %get-tuple-element.27), channel_id=1, source_target_pairs={{1,0},{2,1},{3,2},{4,3},{5,4},{6,5},{7,6},{8,7},{9,8},{10,9},{11,1... | collective-permute-start | bytes 983048 | tf_op jit(solution)/shard_map/ppermute | solution.py:396
  133.0 16.5 %all-to-all-start.1 = ((f32[32,1,128]{2,1,0:T(1,128)}), f32[32,1,128]{2,1,0:T(1,128)S(1)}, u32[]{:S(2)}, u32[]{:S(2)}) async-start(f32[32,1,128]{2,1,0:T(1,128)} %bitcast.7), calls=%async_computation.1 | async-start | bytes 32768 | tf_op jit(solution)/shard_map/all_to_all | solution.py:339
  149.5 5.2 %copy-start = (bf16[9,1280,640]{2,1,0:T(8,128)(2,1)S(1)}, bf16[9,1280,640]{2,1,0:T(8,128)(2,1)}, u32[]{:S(2)}) copy-start(bf16[9,1280,640]{2,1,0:T(8,128)(2,1)} %w_ref.3) | copy-start | bytes 44236804
